TPU v7x, 32 devices: a whole 2x2x4 slice. The times are simulated.
32 devices in a mesh: tm: 2 (over x), ha: 4 (over z), wa: 4 (over y, core).
Axes of the slice: x: 2, y: 2, z: 4, core: 2. Of those that a mesh axis runs over, the one named last changes fastest.
Arguments:
- frames: bfloat16 [2, 128, 256, 128], P('tm', 'ha', 'wa'), may hold values from -24 to 24
- conv_first: bfloat16 [3, 3, 128, 128], replicated, may hold values from -0.1875 to 0.1875
- conv_second: bfloat16 [3, 3, 128, 128], replicated, may hold values from -0.1875 to 0.1875
- norm_attn: float32 [128], replicated, may hold values from 0.25 to 1.75
- qkv_weight: bfloat16 [128, 384], replicated, may hold values from -0.81 to 0.81
- out_weight: bfloat16 [128, 128], replicated, may hold values from -0.5 to 0.5
- norm_mlp: float32 [128], replicated, may hold values from 0.25 to 1.75
- mlp_in: bfloat16 [128, 512], replicated, may hold values from -0.5 to 0.5
- mlp_out: bfloat16 [512, 128], replicated, may hold values from -0.25 to 0.25
- target: bfloat16 [128, 256, 2, 128], P(('ha', 'tm'), 'wa'), may hold values from -18 to 18
Outputs:
- predicted: bfloat16 [128, 256, 2, 128], P(('ha', 'tm'), 'wa')
- loss: float32 [], replicated
All inputs are finite; a program needn't handle non-finite values.
Results may differ from a plain program's by a relative error of at most 0.014.
Values may be sent and summed in bfloat16 or wider, within the bound.
A program may use at most 128 MiB of HBM per device.

v0:
```python
import jax
import jax.numpy as jnp
from jax import lax
from jax.experimental import pallas as pl
from jax.experimental.pallas import tpu as pltpu
from jax.sharding import PartitionSpec as P

HEADS = 4
RADIUS = 4


EPSILON = 1e-06


def shifted(value, axis, steps):
    count = lax.axis_size(axis)
    initial, last = (max(0, -steps), min(count, count - steps))
    return lax.ppermute(value, axis, [(source, source + steps) for source in range(initial, last)])


def with_halo(block, sides, width):
    for axis, dim in sides:
        count = lax.axis_size(axis)
        forward = [(i, i + 1) for i in range(count - 1)]
        backward = [(target, source) for source, target in forward]
        low = lax.ppermute(
            lax.slice_in_dim(block, block.shape[dim] - width, None, axis=dim), axis, forward
        )
        high = lax.ppermute(lax.slice_in_dim(block, 0, width, axis=dim), axis, backward)
        block = jnp.concatenate([low, block, high], axis=dim)
    return block


def convolve(padded, kernel, row_count, col_count):
    nframes = padded.shape[0]
    summed = jnp.zeros((nframes * row_count * col_count, kernel.shape[3]), jnp.float32)
    for tap_row in range(3):
        for tap_col in range(3):
            patch = padded[:, tap_row : tap_row + row_count, tap_col : tap_col + col_count]
            summed = summed + jnp.dot(
                patch.reshape(-1, patch.shape[3]),
                kernel[tap_row, tap_col],
                preferred_element_type=jnp.float32,
            )
    return summed.reshape(nframes, row_count, col_count, -1)


def correlate(current, windowed):
    nframes, tile_rows, tile_cols, channels = current.shape
    span = 2 * RADIUS + 1
    reach = tile_cols + 2 * RADIUS
    col_here = jnp.arange(tile_cols)[:, None, None]
    col_there = jnp.arange(reach)[None, :, None]
    offsets = jnp.arange(span)[None, None, :]
    band = col_there == col_here + offsets
    band_f32 = band.astype(jnp.float32)
    band_bf16 = band.astype(jnp.bfloat16)
    pieces = []
    for shift_row in range(span):
        rows_window = windowed[:, shift_row : shift_row + tile_rows]
        banded = jnp.einsum(
            "fhic,fhjc->fhij", current, rows_window, preferred_element_type=jnp.float32
        )
        pieces.append(
            jnp.einsum("fhij,ijb->fhib", banded, band_f32, precision=lax.Precision.HIGHEST)
        )
    scores = jnp.concatenate(pieces, axis=-1) * channels ** (-0.5)
    top = jnp.max(scores, axis=-1, keepdims=True)
    expo = jnp.exp(scores - top)
    probs = (expo / jnp.sum(expo, axis=-1, keepdims=True)).astype(jnp.bfloat16)
    gathered = jnp.zeros(current.shape, jnp.float32)
    for shift_row in range(span):
        rows_window = windowed[:, shift_row : shift_row + tile_rows]
        chosen = probs[..., shift_row * span : (shift_row + 1) * span]
        spread = jnp.einsum(
            "fhib,ijb->fhij", chosen, band_bf16, preferred_element_type=jnp.float32
        ).astype(jnp.bfloat16)
        gathered = gathered + jnp.einsum(
            "fhij,fhjc->fhic", spread, rows_window, preferred_element_type=jnp.float32
        )
    return (current.astype(jnp.float32) + gathered).astype(jnp.bfloat16)


def project(series, norm_attn, qkv_weight):
    npos, nframes, channels = series.shape
    base = series.astype(jnp.float32)
    normed = (
        base * lax.rsqrt(jnp.mean(base * base, axis=-1, keepdims=True) + EPSILON) * norm_attn
    ).astype(jnp.bfloat16)
    projected = jnp.dot(
        normed.reshape(-1, channels), qkv_weight, preferred_element_type=jnp.float32
    ).astype(jnp.bfloat16)
    projected = projected.reshape(npos, nframes, 3 * channels)
    return (
        projected[..., :channels],
        projected[..., channels : 2 * channels],
        projected[..., 2 * channels :],
    )


def attend(queries, key_rows, value_rows, query_ids, key_ids):
    npos, query_count, channels = queries.shape
    key_count = key_rows.shape[1]
    depth = channels // HEADS
    query_heads = queries.reshape(npos, query_count, HEADS, depth)
    key_heads = key_rows.reshape(npos, key_count, HEADS, depth)
    value_heads = value_rows.reshape(npos, key_count, HEADS, depth)
    scores = jnp.einsum(
        "pqhd,pkhd->phqk", query_heads, key_heads, preferred_element_type=jnp.float32
    ) * depth ** (-0.5)
    allowed = key_ids[None, :] <= query_ids[:, None]
    scores = jnp.where(allowed, scores, -1e30)
    top = jnp.max(scores, axis=-1, keepdims=True)
    expo = jnp.exp(scores - top)
    weights = (expo / jnp.sum(expo, axis=-1, keepdims=True)).astype(jnp.bfloat16)
    attended = jnp.einsum(
        "phqk,pkhd->pqhd", weights, value_heads, preferred_element_type=jnp.float32
    )
    return attended.reshape(npos, query_count, channels).astype(jnp.bfloat16)


def finish(series, attended, out_weight, norm_mlp, mlp_in, mlp_out):
    npos, nframes, channels = series.shape
    resid = series.astype(jnp.float32) + jnp.dot(
        attended.reshape(-1, channels), out_weight, preferred_element_type=jnp.float32
    ).reshape(npos, nframes, channels)
    mlp_input = (
        resid * lax.rsqrt(jnp.mean(resid * resid, axis=-1, keepdims=True) + EPSILON) * norm_mlp
    ).astype(jnp.bfloat16)
    mlp_hidden = jax.nn.gelu(
        jnp.dot(mlp_input.reshape(-1, channels), mlp_in, preferred_element_type=jnp.float32)
    ).astype(jnp.bfloat16)
    output = resid + jnp.dot(mlp_hidden, mlp_out, preferred_element_type=jnp.float32).reshape(
        npos, nframes, channels
    )
    return output.astype(jnp.bfloat16)


def shards(
    frames,
    conv_first,
    conv_second,
    norm_attn,
    qkv_weight,
    out_weight,
    norm_mlp,
    mlp_in,
    mlp_out,
    target,
):
    frame_count, tile_rows, tile_cols, channels = frames.shape
    arrival = shifted(frames, "tm", -1)
    following = jnp.concatenate([frames[1:], arrival], axis=0)
    windowed = with_halo(following, (("ha", 1), ("wa", 2)), RADIUS)
    blended = correlate(frames, windowed)
    padded_first = with_halo(blended, (("ha", 1), ("wa", 2)), 1)
    hidden_map = jax.nn.gelu(convolve(padded_first, conv_first, tile_rows, tile_cols)).astype(
        jnp.bfloat16
    )
    hidden_map = with_halo(hidden_map, (("ha", 1), ("wa", 2)), 1)
    encoded = (
        blended.astype(jnp.float32) + convolve(hidden_map, conv_second, tile_rows, tile_cols)
    ).astype(jnp.bfloat16)
    series = jnp.transpose(
        lax.all_to_all(encoded, "tm", split_axis=1, concat_axis=0, tiled=True), (1, 2, 0, 3)
    )
    layout = series.shape
    tokens_flat = series.reshape(-1, layout[2], layout[3])
    frame_ids = jnp.arange(layout[2])
    queries, key_rows, value_rows = project(tokens_flat, norm_attn, qkv_weight)
    attended = attend(queries, key_rows, value_rows, frame_ids, frame_ids)
    predicted = finish(tokens_flat, attended, out_weight, norm_mlp, mlp_in, mlp_out).reshape(layout)
    errors = predicted.astype(jnp.float32) - target.astype(jnp.float32)
    summed = lax.psum(jnp.sum(errors * errors), ("tm", "ha", "wa"))
    entries = predicted.size * lax.axis_size("tm") * lax.axis_size("ha") * lax.axis_size("wa")
    return (predicted, summed / entries)


RIMS = (2, RADIUS + 2)
SIDE = 16
QROWS = 10
QCOLS = 16


def window_parts(frame, place, tile_rows, tile_cols):
    rim = RIMS[frame]
    main = tile_rows // 2 + rim
    if place == 0:
        rows = [(0, main, rim, 0), (tile_rows - rim, rim, 0, -1)]
    else:
        rows = [(tile_rows - main, main, 0, 0), (0, rim, main, 1)]
    cols = [
        (0, tile_cols, SIDE, 0),
        (tile_cols - SIDE, SIDE, 0, -1),
        (0, SIDE, SIDE + tile_cols, 1),
    ]
    return [(row, col) for row in rows for col in cols]


def gather_kernel(
    ha_count, wa_count, frames_ref, win0, win1, send_sem, recv_sem
):
    wins = (win0, win1)
    _, tile_rows, tile_cols, _ = frames_ref.shape
    here_t, here_a, here_w = (lax.axis_index(n) for n in ("tm", "ha", "wa"))
    barrier = pltpu.get_barrier_semaphore()

    def inside(a, w):
        return (a >= 0) & (a < ha_count) & (w >= 0) & (w < wa_count)

    def device(t, a, w):
        wrapped = (lax.rem(a + ha_count, ha_count), lax.rem(w + wa_count, wa_count))
        return (jnp.int32(t), *wrapped)

    def branch(mine):
        other = 1 - mine
        expected = jnp.int32(0)
        for frame in range(2):
            for row, col in window_parts(frame, mine, tile_rows, tile_cols):
                a, w = here_a + row[3], here_w + col[3]
                if frame == mine and row[3] == 0 and col[3] == 0:
                    continue

                @pl.when(inside(a, w))
                def _():
                    pl.semaphore_signal(
                        barrier,
                        inc=1,
                        device_id=device(frame, a, w),
                        device_id_type=pl.DeviceIdType.MESH,
                    )

        sends = []
        for place in range(2):
            for slot, (row, col) in enumerate(
                window_parts(mine, place, tile_rows, tile_cols)
            ):
                a, w = here_a - row[3], here_w - col[3]
                local = place == mine and row[3] == 0 and col[3] == 0
                source = frames_ref.at[0, pl.ds(row[0], row[1]), pl.ds(col[0], col[1])]
                target = wins[mine].at[pl.ds(row[2], row[1]), pl.ds(col[2], col[1])]
                if local:
                    own = pltpu.make_async_copy(source, target, recv_sem.at[mine * 6 + slot])
                    continue
                expected = expected + inside(a, w).astype(jnp.int32)
                sends.append(
                    (
                        inside(a, w),
                        pltpu.make_async_remote_copy(
                            src_ref=source,
                            dst_ref=target,
                            send_sem=send_sem.at[place * 6 + slot],
                            recv_sem=recv_sem.at[mine * 6 + slot],
                            device_id=device(place, a, w),
                            device_id_type=pl.DeviceIdType.MESH,
                        ),
                    )
                )
        own.start()
        arrivals = []
        for frame in range(2):
            for slot, (row, col) in enumerate(
                window_parts(frame, mine, tile_rows, tile_cols)
            ):
                a, w = here_a + row[3], here_w + col[3]
                if frame == mine and row[3] == 0 and col[3] == 0:
                    continue
                target = wins[frame].at[pl.ds(row[2], row[1]), pl.ds(col[2], col[1])]

                def clear(target=target):
                    target[...] = jnp.zeros(target.shape, target.dtype)

                arrival = pltpu.make_async_remote_copy(
                    src_ref=target,
                    dst_ref=target,
                    send_sem=send_sem.at[frame * 6 + slot],
                    recv_sem=recv_sem.at[frame * 6 + slot],
                    device_id=device(other, here_a, here_w),
                    device_id_type=pl.DeviceIdType.MESH,
                )
                arrivals.append((inside(a, w), arrival))
                pl.when(jnp.logical_not(inside(a, w)))(clear)
        pl.semaphore_wait(barrier, expected)
        for exists, copy in sends:
            pl.when(exists)(copy.start)
        own.wait()
        for exists, arrival in arrivals:
            pl.when(exists)(arrival.wait_recv)
        for exists, copy in sends:
            pl.when(exists)(copy.wait_send)

    pl.when(here_t == 0)(lambda: branch(0))
    pl.when(here_t == 1)(lambda: branch(1))


def gather_windows(frames):
    _, tile_rows, tile_cols, channels = frames.shape
    shapes = [
        jax.ShapeDtypeStruct(
            (tile_rows // 2 + 2 * rim, tile_cols + 2 * SIDE, channels), frames.dtype
        )
        for rim in RIMS
    ]
    ha_count, wa_count = lax.axis_size("ha"), lax.axis_size("wa")

    def kernel(*refs):
        gather_kernel(ha_count, wa_count, *refs)

    return pl.pallas_call(
        kernel,
        out_shape=shapes,
        in_specs=[pl.BlockSpec(memory_space=pl.ANY)],
        out_specs=[pl.BlockSpec(memory_space=pltpu.VMEM)] * 2,
        scratch_shapes=[
            pltpu.SemaphoreType.DMA((12,)),
            pltpu.SemaphoreType.DMA((12,)),
        ],
        compiler_params=pltpu.CompilerParams(collective_id=0, has_side_effects=True),
    )(frames)


def rounded(value):
    return value.astype(jnp.bfloat16)


def predict_kernel(
    ha_count,
    wa_count,
    win0,
    win1,
    conv_first,
    conv_second,
    norm_attn,
    qkv_weight,
    out_weight,
    norm_mlp,
    mlp_in,
    mlp_out,
    target,
    predicted,
    loss,
    bias,
    blended,
    patches,
    hidden,
    patches_hidden,
    encoded,
    paired,
):
    row_count = win0.shape[0] - 2 * RIMS[0]
    width = win0.shape[1]
    col_count = width - 2 * SIDE
    channels = win0.shape[2]
    here_t, here_a, here_w = (lax.axis_index(n) for n in ("tm", "ha", "wa"))
    first_row = (here_a * 2 + here_t) * row_count
    first_col = here_w * col_count
    image_rows = ha_count * 2 * row_count
    image_cols = wa_count * col_count

    def in_image(shape, row_start, col_start):
        row = lax.broadcasted_iota(jnp.int32, shape, 0) + row_start
        col = lax.broadcasted_iota(jnp.int32, shape, 1) + col_start
        return (row >= 0) & (row < image_rows) & (col >= 0) & (col < image_cols)

    krows, kcols = QROWS + 2 * RADIUS, QCOLS + 16
    queries_n, keys_n = QROWS * QCOLS, krows * kcols
    q_at = lax.broadcasted_iota(jnp.int32, (queries_n, keys_n), 0)
    k_at = lax.broadcasted_iota(jnp.int32, (queries_n, keys_n), 1)
    d_row = k_at // kcols - q_at // QCOLS
    d_col = k_at % kcols - q_at % QCOLS - (8 - RADIUS)
    near = (d_row >= 0) & (d_row <= 2 * RADIUS) & (d_col >= 0) & (d_col <= 2 * RADIUS)
    bias[...] = jnp.where(near, 0.0, -1e30)
    scale = channels ** (-0.5) * 1.4426950408889634

    @pl.loop(0, win0.shape[0] // QROWS)
    def _(step):
        top_row = step * QROWS
        for start in range(8, width - 8, QCOLS):
            query = win0[pl.ds(top_row, QROWS), start : start + QCOLS].reshape(
                queries_n, channels
            )
            keys = win1[pl.ds(top_row, krows), start - 8 : start + QCOLS + 8].reshape(
                keys_n, channels
            )
            scores = lax.dot_general(
                query, keys, (((1,), (1,)), ((), ())), preferred_element_type=jnp.float32
            )
            scores = scores * scale + bias[...]
            expo = jnp.exp2(scores - jnp.max(scores, axis=-1, keepdims=True))
            total = jnp.sum(expo, axis=-1, keepdims=True)
            found = jnp.dot(rounded(expo), keys, preferred_element_type=jnp.float32) / total
            mixed = rounded(query.astype(jnp.float32) + found).astype(jnp.float32)
            mixed = mixed.reshape(QROWS, QCOLS, channels)
            keep = in_image(
                mixed.shape, first_row - RIMS[0] + top_row, first_col - SIDE + start
            )
            blended[pl.ds(top_row, QROWS), start : start + QCOLS] = jnp.where(keep, mixed, 0.0)

    for frame in range(2):
        if frame == 1:
            gap = RIMS[1] - RIMS[0]
            blended[...] = win1[gap : gap + win0.shape[0]].astype(jnp.float32)
        for tap in range(3):
            patches[:, :, tap * channels : (tap + 1) * channels] = rounded(
                blended[:, 7 + tap : width - 9 + tap]
            )

        @pl.loop(0, (row_count + 2) // 6)
        def _(step):
            at = step * 6
            lhs = jnp.concatenate([patches[pl.ds(at + i, 6)] for i in range(3)], axis=-1)
            shape = (6, width - 16, channels)
            out = jnp.dot(
                lhs.reshape(-1, 9 * channels), conv_first[...], preferred_element_type=jnp.float32
            )
            out = rounded(jax.nn.gelu(out)).astype(jnp.float32).reshape(shape)
            keep = in_image(shape, first_row - 1 + at, first_col - 8)
            hidden[pl.ds(at, 6)] = jnp.where(keep, out, 0.0)

        for tap in range(3):
            patches_hidden[:, :, tap * channels : (tap + 1) * channels] = rounded(
                hidden[:, 7 + tap : 7 + tap + col_count]
            )

        @pl.loop(0, row_count // 8)
        def _(step):
            at = step * 8
            lhs = jnp.concatenate([patches_hidden[pl.ds(at + i, 8)] for i in range(3)], axis=-1)
            out = jnp.dot(
                lhs.reshape(-1, 9 * channels), conv_second[...], preferred_element_type=jnp.float32
            )
            base = blended[pl.ds(at + 2, 8), SIDE : SIDE + col_count].reshape(out.shape)
            encoded[frame, pl.ds(at * col_count, 8 * col_count)] = rounded(base + out).astype(
                jnp.float32
            )

    depth = channels // HEADS
    lane_in = lax.broadcasted_iota(jnp.int32, (2 * channels, channels), 0) % channels
    lane_out = lax.broadcasted_iota(jnp.int32, (2 * channels, channels), 1)
    head_sum = rounded(jnp.where(lane_in // depth == lane_out // depth, 1.0, 0.0))
    chunk = 256

    def unit(value, gain):
        mean = jnp.mean(value * value, axis=-1, keepdims=True)
        return rounded(value * lax.rsqrt(mean + EPSILON) * gain[...])

    def dot(left, right):
        return jnp.dot(left, right, preferred_element_type=jnp.float32)

    @pl.loop(0, row_count * col_count // chunk, init_carry=jnp.zeros((8, channels), jnp.float32))
    def errors(step, carry):
        at = pl.multiple_of(step * chunk, chunk)
        series = jnp.concatenate([encoded[0, pl.ds(at, chunk)], encoded[1, pl.ds(at, chunk)]])
        projected = rounded(dot(unit(series, norm_attn), qkv_weight[...])).astype(jnp.float32)
        query = projected[chunk:, :channels]
        keys = projected[:, channels : 2 * channels]
        values = projected[:, 2 * channels :]
        product = query * (keys[chunk:] - keys[:chunk])
        high = rounded(product)
        low = rounded(product - high.astype(jnp.float32))
        gap = dot(jnp.concatenate([high, low], axis=-1), head_sum) * depth ** (-0.5)
        half = 0.5 * jnp.tanh(0.5 * gap)
        weight_now = rounded(0.5 + half).astype(jnp.float32)
        weight_past = rounded(0.5 - half).astype(jnp.float32)
        attended = weight_past * values[:chunk] + weight_now * values[chunk:]
        attended = rounded(jnp.concatenate([values[:chunk], attended]))
        resid = series + dot(attended, out_weight[...])
        inner = rounded(jax.nn.gelu(dot(unit(resid, norm_mlp), mlp_in[...])))
        output = resid + dot(inner, mlp_out[...])
        paired[pl.ds(0, chunk, stride=2)] = output[:chunk]
        paired[pl.ds(1, chunk, stride=2)] = output[chunk:]
        final = rounded(paired[...])
        both = pl.ds(pl.multiple_of(2 * at, 2 * chunk), 2 * chunk)
        predicted[both] = final
        error = final.astype(jnp.float32) - target[both].astype(jnp.float32)
        return carry + jnp.sum((error * error).reshape(-1, 8, channels), axis=0)

    loss[...] = errors


def predict(win0, win1, weights, target):
    row_count = win0.shape[0] - 2 * RIMS[0]
    width, channels = win0.shape[1:]
    col_count = width - 2 * SIDE
    ha_count, wa_count = lax.axis_size("ha"), lax.axis_size("wa")

    def kernel(*refs):
        predict_kernel(ha_count, wa_count, *refs)

    tokens = 2 * row_count * col_count
    operands = (win0, win1, *weights, target)
    return pl.pallas_call(
        kernel,
        out_shape=[
            jax.ShapeDtypeStruct((tokens, channels), jnp.bfloat16),
            jax.ShapeDtypeStruct((8, channels), jnp.float32),
        ],
        in_specs=[pl.BlockSpec(memory_space=pltpu.VMEM)] * len(operands),
        out_specs=[pl.BlockSpec(memory_space=pltpu.VMEM)] * 2,
        scratch_shapes=[
            pltpu.VMEM((QROWS * QCOLS, (QROWS + 2 * RADIUS) * (QCOLS + 16)), jnp.float32),
            pltpu.VMEM((row_count + 4, width, channels), jnp.float32),
            pltpu.VMEM((row_count + 4, width - 16, 3 * channels), jnp.bfloat16),
            pltpu.VMEM((row_count + 2, width - 16, channels), jnp.float32),
            pltpu.VMEM((row_count + 2, col_count, 3 * channels), jnp.bfloat16),
            pltpu.VMEM((2, row_count * col_count, channels), jnp.float32),
            pltpu.VMEM((512, channels), jnp.float32),
        ],
        compiler_params=pltpu.CompilerParams(vmem_limit_bytes=48 * 1024 * 1024),
    )(*operands)


def pair_shards(
    frames,
    conv_first,
    conv_second,
    norm_attn,
    qkv_weight,
    out_weight,
    norm_mlp,
    mlp_in,
    mlp_out,
    target,
):
    channels = frames.shape[3]
    win0, win1 = gather_windows(frames)
    weights = (
        conv_first.reshape(-1, channels),
        conv_second.reshape(-1, channels),
        norm_attn.reshape(1, channels),
        qkv_weight,
        out_weight,
        norm_mlp.reshape(1, channels),
        mlp_in,
        mlp_out,
    )
    predicted, errors = predict(win0, win1, weights, target.reshape(-1, channels))
    summed = lax.psum(jnp.sum(errors), ("tm", "ha", "wa"))
    entries = target.size * lax.axis_size("tm") * lax.axis_size("ha") * lax.axis_size("wa")
    return (predicted.reshape(target.shape), summed / entries)


def solution(mesh):
    in_specs = (
        P("tm", "ha", "wa", None),
        P(),
        P(),
        P(),
        P(),
        P(),
        P(),
        P(),
        P(),
        P(("ha", "tm"), "wa", None, None),
    )
    out_specs = (P(("ha", "tm"), "wa", None, None), P())
    body = pair_shards if mesh.shape["tm"] == 2 else shards
    return jax.shard_map(body, mesh=mesh, in_specs=in_specs, out_specs=out_specs, check_vma=False)
```

profile of v0, /device:TPU:0, one launch (start us, length us, event | category | flops | bytes accessed | tf_op | source)
XLA Modules:
  0.0 87.1 jit_solution(6375169890538647737)
XLA Ops:
  0.6 0.0 copy-start.1
  0.6 18.2 %shard_map.113 = (bf16[20,96,128]{2,1,0:T(8,128)(2,1)}, bf16[28,96,128]{2,1,0:T(8,128)(2,1)}) custom-call(bf16[1,32,64,128]{3,2,1,0:T(8,128)(2,1)} %refs_0_.1), custom_call_target="tpu_custom_call" | custom-call | tf_op jit(solution)/shard_map/pallas_call | solution.py:309
  18.9 0.0 copy-start.9
  18.9 0.0 copy-start.10
  18.9 0.0 copy-done.1
  18.9 0.6 copy-done.9
  19.5 0.0 copy-done.10
  19.5 0.0 copy-start
  19.6 1.1 %copy-done = bf16[28,96,128]{2,1,0:T(8,128)(2,1)S(1)} copy-done((bf16[28,96,128]{2,1,0:T(8,128)(2,1)S(1)}, bf16[28,96,128]{2,1,0:T(8,128)(2,1)}, u32[]{:S(2)}) %copy-start) | copy-done | bytes 688152
  20.6 0.0 copy-start.2
  20.7 1.0 %copy-done.2 = bf16[20,96,128]{2,1,0:T(8,128)(2,1)S(1)} copy-done((bf16[20,96,128]{2,1,0:T(8,128)(2,1)S(1)}, bf16[20,96,128]{2,1,0:T(8,128)(2,1)}, u32[]{:S(2)}) %copy-start.2) | copy-done | bytes 491544
  21.7 0.0 copy-start.3
  21.7 1.0 %copy-done.3 = bf16[3,3,128,128]{3,2,1,0:T(8,128)(2,1)S(1)} copy-done((bf16[3,3,128,128]{3,2,1,0:T(8,128)(2,1)S(1)}, bf16[3,3,128,128]{3,2,1,0:T(8,128)(2,1)}, u32[]{:S(2)}) %copy-start.3) | copy-done | bytes 294936
  22.6 0.0 copy-start.4
  22.6 1.0 %copy-done.4 = bf16[3,3,128,128]{3,2,1,0:T(8,128)(2,1)S(1)} copy-done((bf16[3,3,128,128]{3,2,1,0:T(8,128)(2,1)S(1)}, bf16[3,3,128,128]{3,2,1,0:T(8,128)(2,1)}, u32[]{:S(2)}) %copy-start.4) | copy-done | bytes 294936
  23.6 0.0 copy-start.5
  23.6 0.9 %copy-done.5 = bf16[128,512]{1,0:T(8,128)(2,1)S(1)} copy-done((bf16[128,512]{1,0:T(8,128)(2,1)S(1)}, bf16[128,512]{1,0:T(8,128)(2,1)}, u32[]{:S(2)}) %copy-start.5) | copy-done | bytes 131096
  24.5 0.0 copy-start.6
  24.5 0.9 %copy-done.6 = bf16[512,128]{1,0:T(8,128)(2,1)S(1)} copy-done((bf16[512,128]{1,0:T(8,128)(2,1)S(1)}, bf16[512,128]{1,0:T(8,128)(2,1)}, u32[]{:S(2)}) %copy-start.6) | copy-done | bytes 131096
  25.4 0.9 %copy-done.7 = bf16[128,384]{1,0:T(8,128)(2,1)S(1)} copy-done((bf16[128,384]{1,0:T(8,128)(2,1)S(1)}, bf16[128,384]{1,0:T(8,128)(2,1)}, u32[]{:S(2)}) %copy-start.7) | copy-done | bytes 98328
  26.3 0.8 copy-done.8
  27.1 15.1 %shard_map.114 = (bf16[2048,128]{1,0:T(8,128)(2,1)}, f32[8,128]{1,0:T(8,128)S(1)}) custom-call(bf16[20,96,128]{2,1,0:T(8,128)(2,1)S(1)} %copy-done.2, bf16[28,96,128]{2,1,0:T(8,128)(2,1)S(1)} %copy-done, bf16[1152,128]{1,0:T(8,128)(2,1)S(1)} %bitcast.7, bf16[1152,128]{1,0:T(8,128)(2,1)S(1)} %bitcast.8, f32[1,128]{1,0:T(1,128)S(1)} %bitcast.9, ...), custom_call_target="tpu_custom_call" | custom-call | tf_op jit(solution)/shard_map/pallas_call | solution.py:492
  42.1 0.6 reduce_sum.9
  42.7 42.5 %psum.7 = f32[]{:T(128)} all-reduce(f32[]{:T(128)} %reduce_sum.9), channel_id=1, replica_groups=mesh['tm'=2,'ha'=4,'wa'=4] {'tm','ha','wa'}, use_global_device_ids=true, to_apply=%region_1.0 | all-reduce | flops 1 | bytes 8 | tf_op jit(solution)/shard_map/psum | solution.py:538
  (2 shorter events, 0.0 us)
Async XLA Ops:
  0.6 18.3 %copy-start.1 = (bf16[16,64,2,128]{3,2,1,0:T(2,128)(2,1)S(1)}, bf16[16,64,2,128]{3,2,1,0:T(2,128)(2,1)}, u32[]{:S(2)}) copy-start(bf16[16,64,2,128]{3,2,1,0:T(2,128)(2,1)} %param.19) | copy-start | bytes 1572868
  18.9 0.7 copy-start.9
  18.9 0.7 copy-start.10
  19.5 1.1 %copy-start = (bf16[28,96,128]{2,1,0:T(8,128)(2,1)S(1)}, bf16[28,96,128]{2,1,0:T(8,128)(2,1)}, u32[]{:S(2)}) copy-start(bf16[28,96,128]{2,1,0:T(8,128)(2,1)} %get-tuple-element.7.refs_1_) | copy-start | bytes 2064388
  20.6 1.0 %copy-start.2 = (bf16[20,96,128]{2,1,0:T(8,128)(2,1)S(1)}, bf16[20,96,128]{2,1,0:T(8,128)(2,1)}, u32[]{:S(2)}) copy-start(bf16[20,96,128]{2,1,0:T(8,128)(2,1)} %get-tuple-element.6.refs_0_) | copy-start | bytes 1474564
  21.7 1.0 %copy-start.3 = (bf16[3,3,128,128]{3,2,1,0:T(8,128)(2,1)S(1)}, bf16[3,3,128,128]{3,2,1,0:T(8,128)(2,1)}, u32[]{:S(2)}) copy-start(bf16[3,3,128,128]{3,2,1,0:T(8,128)(2,1)} %param.11) | copy-start | bytes 884740
  22.6 1.0 %copy-start.4 = (bf16[3,3,128,128]{3,2,1,0:T(8,128)(2,1)S(1)}, bf16[3,3,128,128]{3,2,1,0:T(8,128)(2,1)}, u32[]{:S(2)}) copy-start(bf16[3,3,128,128]{3,2,1,0:T(8,128)(2,1)} %param.12) | copy-start | bytes 884740
  23.6 0.9 %copy-start.5 = (bf16[128,512]{1,0:T(8,128)(2,1)S(1)}, bf16[128,512]{1,0:T(8,128)(2,1)}, u32[]{:S(2)}) copy-start(bf16[128,512]{1,0:T(8,128)(2,1)} %refs_8_.1) | copy-start | bytes 393220
  24.5 0.9 %copy-start.6 = (bf16[512,128]{1,0:T(8,128)(2,1)S(1)}, bf16[512,128]{1,0:T(8,128)(2,1)}, u32[]{:S(2)}) copy-start(bf16[512,128]{1,0:T(8,128)(2,1)} %refs_9_.1) | copy-start | bytes 393220
  25.4 0.9 %copy-start.7 = (bf16[128,384]{1,0:T(8,128)(2,1)S(1)}, bf16[128,384]{1,0:T(8,128)(2,1)}, u32[]{:S(2)}) copy-start(bf16[128,384]{1,0:T(8,128)(2,1)} %refs_5_.1) | copy-start | bytes 294916
  26.3 0.8 copy-start.8
where the time goes:
time: 87.6 us; the launch traced here: 87.1 us
  blocking collectives  42.5 us (49%)
  Pallas kernels  33.3 us (38%)
  local copies, waits for them, and re-layouts  8.16 us (9%)
  between operations  2.46 us (3%)
    psum x1, blocking collectives, pair_shards(): summed = lax.psum(jnp.sum(errors), ('tm', 'ha', 'wa'))  42.5 us
    pallas_call x1, Pallas kernels, gather_windows(): pl.pallas_call(kernel, out_shape=shapes, in_specs=[pl.BlockSpec(memory_sp...  18.2 us
    pallas_call x1, Pallas kernels, predict(): pl.pallas_call(kernel, out_shape=[jax.ShapeDtypeStruct((tokens, channels)...  15.1 us
    unnamed x22, local copies, waits for them, and re-layouts  8.16 us

commit v1 on v0

--- a/solution.py
+++ b/solution.py
@@ -506,8 +506,86 @@
             pltpu.VMEM((2, row_count * col_count, channels), jnp.float32),
             pltpu.VMEM((512, channels), jnp.float32),
         ],
-        compiler_params=pltpu.CompilerParams(vmem_limit_bytes=48 * 1024 * 1024),
+        compiler_params=pltpu.CompilerParams(vmem_limit_bytes=60 * 1024 * 1024),
     )(*operands)
+
+
+def total_kernel(
+    wa_count, ha_count, near_count, scale, errors, total, near, part, far, near_sems, far_sems
+):
+    here_t, here_a, here_w = (lax.axis_index(n) for n in ("tm", "ha", "wa"))
+    here = here_t * wa_count + here_w
+
+    def near_peer(step):
+        slot = lax.rem(here + step, near_count)
+        return slot, (slot // wa_count, here_a, lax.rem(slot, wa_count))
+
+    def far_peer(step):
+        slot = lax.rem(here_a + step, ha_count)
+        return slot, (here_t, slot, here_w)
+
+    barrier = pltpu.get_barrier_semaphore()
+    groups = ((near_peer, near_count), (far_peer, ha_count))
+    for peer, count in groups:
+        for step in range(1, count):
+            pl.semaphore_signal(
+                barrier,
+                inc=1,
+                device_id=peer(step)[1],
+                device_id_type=pl.DeviceIdType.MESH,
+            )
+    pl.semaphore_wait(barrier, near_count + ha_count - 2)
+
+    def exchange(source, slots, sems, peer, count, own):
+        def copy(step, slot, device):
+            return pltpu.make_async_remote_copy(
+                src_ref=source,
+                dst_ref=slots.at[slot],
+                send_sem=sems.at[0, step],
+                recv_sem=sems.at[1, slot],
+                device_id=device,
+                device_id_type=pl.DeviceIdType.MESH,
+            )
+
+        for step in range(1, count):
+            copy(step, own, peer(step)[1]).start()
+        slots[own] = source[...]
+        for step in range(1, count):
+            slot, device = peer(step)
+            copy(step, slot, device).wait_recv()
+        for step in range(1, count):
+            copy(step, own, peer(step)[1]).wait_send()
+        summed = slots[0]
+        for slot in range(1, count):
+            summed = summed + slots[slot]
+        return summed
+
+    part[...] = exchange(errors, near, near_sems, near_peer, near_count, here)
+    summed = exchange(part, far, far_sems, far_peer, ha_count, here_a)
+    total[0, 0] = jnp.sum(summed) * scale
+
+
+def total_error(errors, entries):
+    ha_count, wa_count = lax.axis_size("ha"), lax.axis_size("wa")
+    near_count = lax.axis_size("tm") * wa_count
+
+    def kernel(*refs):
+        total_kernel(wa_count, ha_count, near_count, 1.0 / entries, *refs)
+
+    return pl.pallas_call(
+        kernel,
+        out_shape=jax.ShapeDtypeStruct((1, 1), jnp.float32),
+        in_specs=[pl.BlockSpec(memory_space=pltpu.VMEM)],
+        out_specs=pl.BlockSpec(memory_space=pltpu.SMEM),
+        scratch_shapes=[
+            pltpu.VMEM((near_count, *errors.shape), jnp.float32),
+            pltpu.VMEM(errors.shape, jnp.float32),
+            pltpu.VMEM((ha_count, *errors.shape), jnp.float32),
+            pltpu.SemaphoreType.DMA((2, near_count)),
+            pltpu.SemaphoreType.DMA((2, ha_count)),
+        ],
+        compiler_params=pltpu.CompilerParams(collective_id=1, has_side_effects=True),
+    )(errors)
 
 
 def pair_shards(
@@ -535,9 +613,8 @@
         mlp_out,
     )
     predicted, errors = predict(win0, win1, weights, target.reshape(-1, channels))
-    summed = lax.psum(jnp.sum(errors), ("tm", "ha", "wa"))
     entries = target.size * lax.axis_size("tm") * lax.axis_size("ha") * lax.axis_size("wa")
-    return (predicted.reshape(target.shape), summed / entries)
+    return (predicted.reshape(target.shape), total_error(errors, entries).reshape(()))
 
 
 def solution(mesh):

time: 87.6 us -> 50.7 us (0.58)
  blocking collectives: 42.5 us -> 0 us
  Pallas kernels: 33.3 us -> 48.1 us
  local copies, waits for them, and re-layouts: 8.16 us -> 0 us
    psum x1 -> x0, blocking collectives: 42.5 us -> none  [pair_shards(): summed = lax.psum(jnp.sum(errors), ('tm', 'ha', 'wa'))]
    pallas_call x0 -> x1, Pallas kernels: none -> 13.1 us  [total_error(): pl.pallas_call(kernel, out_shape=jax.ShapeDtypeStruct((1, 1), jnp.float32...]
    unnamed x22 -> x0, local copies, waits for them, and re-layouts: 8.16 us -> none
    pallas_call x1, Pallas kernels: 15.1 us -> 16.8 us  [predict(): pl.pallas_call(kernel, out_shape=[jax.ShapeDtypeStruct((tokens, channels)...]
where the time goes in v1:
time: 50.7 us; the launch traced here: 50.5 us
  Pallas kernels  48.1 us (95%)
  between operations  2.4 us (5%)
    pallas_call x1, Pallas kernels, gather_windows(): pl.pallas_call(kernel, out_shape=shapes, in_specs=[pl.BlockSpec(memory_sp...  18.2 us
    pallas_call x1, Pallas kernels, predict(): pl.pallas_call(kernel, out_shape=[jax.ShapeDtypeStruct((tokens, channels)...  16.8 us
    pallas_call x1, Pallas kernels, total_error(): pl.pallas_call(kernel, out_shape=jax.ShapeDtypeStruct((1, 1), jnp.float32...  13.1 us

profile of v1, /device:TPU:0, one launch (start us, length us, event | category | flops | bytes accessed | tf_op | source)
XLA Modules:
  0.0 50.5 jit_solution(17172848751705473400)
XLA Ops:
  0.6 18.2 %shard_map.113 = (bf16[20,96,128]{2,1,0:T(8,128)(2,1)}, bf16[28,96,128]{2,1,0:T(8,128)(2,1)}) custom-call(bf16[1,32,64,128]{3,2,1,0:T(8,128)(2,1)} %refs_0_.1), custom_call_target="tpu_custom_call" | custom-call | tf_op jit(solution)/shard_map/pallas_call | solution.py:309
  18.8 16.8 %shard_map.114 = (bf16[2048,128]{1,0:T(8,128)(2,1)}, f32[8,128]{1,0:T(8,128)}) custom-call(bf16[20,96,128]{2,1,0:T(8,128)(2,1)} %get-tuple-element.6.refs_0_, bf16[28,96,128]{2,1,0:T(8,128)(2,1)} %get-tuple-element.7.refs_1_, bf16[1152,128]{1,0:T(8,128)(2,1)} %bitcast.8, bf16[1152,128]{1,0:T(8,128)(2,1)} %bitcast.9, f32[1,128]{1,0:T(1,128)} %bitcast.10, ...), custom_call_target="tpu_custom_call" | custom-call | tf_op jit(solution)/shard_map/pallas_call | solution.py:492
  35.6 13.1 %shard_map.115 = f32[1,1]{1,0:T(1,128)} custom-call(f32[8,128]{1,0:T(8,128)} %get-tuple-element.9.refs_0_), custom_call_target="tpu_custom_call" | custom-call | tf_op jit(solution)/shard_map/pallas_call | solution.py:575

commit v2 on v1

--- a/solution.py
+++ b/solution.py
@@ -178,7 +178,7 @@
 
 RIMS = (2, RADIUS + 2)
 SIDE = 16
-QROWS = 10
+QROWS = 20
 QCOLS = 16
 
 
@@ -405,17 +405,17 @@
                 blended[:, 7 + tap : width - 9 + tap]
             )
 
-        @pl.loop(0, (row_count + 2) // 6)
+        @pl.loop(0, (row_count + 2) // 9)
         def _(step):
-            at = step * 6
-            lhs = jnp.concatenate([patches[pl.ds(at + i, 6)] for i in range(3)], axis=-1)
-            shape = (6, width - 16, channels)
+            at = step * 9
+            lhs = jnp.concatenate([patches[pl.ds(at + i, 9)] for i in range(3)], axis=-1)
+            shape = (9, width - 16, channels)
             out = jnp.dot(
                 lhs.reshape(-1, 9 * channels), conv_first[...], preferred_element_type=jnp.float32
             )
             out = rounded(jax.nn.gelu(out)).astype(jnp.float32).reshape(shape)
             keep = in_image(shape, first_row - 1 + at, first_col - 8)
-            hidden[pl.ds(at, 6)] = jnp.where(keep, out, 0.0)
+            hidden[pl.ds(at, 9)] = jnp.where(keep, out, 0.0)
 
         for tap in range(3):
             patches_hidden[:, :, tap * channels : (tap + 1) * channels] = rounded(
@@ -438,7 +438,7 @@
     lane_in = lax.broadcasted_iota(jnp.int32, (2 * channels, channels), 0) % channels
     lane_out = lax.broadcasted_iota(jnp.int32, (2 * channels, channels), 1)
     head_sum = rounded(jnp.where(lane_in // depth == lane_out // depth, 1.0, 0.0))
-    chunk = 256
+    chunk = 1024
 
     def unit(value, gain):
         mean = jnp.mean(value * value, axis=-1, keepdims=True)
@@ -504,7 +504,7 @@
             pltpu.VMEM((row_count + 2, width - 16, channels), jnp.float32),
             pltpu.VMEM((row_count + 2, col_count, 3 * channels), jnp.bfloat16),
             pltpu.VMEM((2, row_count * col_count, channels), jnp.float32),
-            pltpu.VMEM((512, channels), jnp.float32),
+            pltpu.VMEM((2048, channels), jnp.float32),
         ],
         compiler_params=pltpu.CompilerParams(vmem_limit_bytes=60 * 1024 * 1024),
     )(*operands)

time: 50.7 us -> 47.7 us (0.941)
  Pallas kernels: 48.1 us -> 45.1 us
    pallas_call x1, Pallas kernels: 16.8 us -> 13.8 us  [predict(): pl.pallas_call(kernel, out_shape=[jax.ShapeDtypeStruct((tokens, channels)...]
where the time goes in v2:
time: 47.7 us; the launch traced here: 47.5 us
  Pallas kernels  45.1 us (95%)
  between operations  2.4 us (5%)
    pallas_call x1, Pallas kernels, gather_windows(): pl.pallas_call(kernel, out_shape=shapes, in_specs=[pl.BlockSpec(memory_sp...  18.2 us
    pallas_call x1, Pallas kernels, predict(): pl.pallas_call(kernel, out_shape=[jax.ShapeDtypeStruct((tokens, channels)...  13.8 us
    pallas_call x1, Pallas kernels, total_error(): pl.pallas_call(kernel, out_shape=jax.ShapeDtypeStruct((1, 1), jnp.float32...  13.1 us

profile of v2, /device:TPU:0, one launch (start us, length us, event | category | flops | bytes accessed | tf_op | source)
XLA Modules:
  0.0 47.5 jit_solution(9477137576325003500)
XLA Ops:
  0.6 18.2 %shard_map.113 = (bf16[20,96,128]{2,1,0:T(8,128)(2,1)}, bf16[28,96,128]{2,1,0:T(8,128)(2,1)}) custom-call(bf16[1,32,64,128]{3,2,1,0:T(8,128)(2,1)} %refs_0_.1), custom_call_target="tpu_custom_call" | custom-call | tf_op jit(solution)/shard_map/pallas_call | solution.py:309
  18.8 13.8 %shard_map.114 = (bf16[2048,128]{1,0:T(8,128)(2,1)}, f32[8,128]{1,0:T(8,128)}) custom-call(bf16[20,96,128]{2,1,0:T(8,128)(2,1)} %get-tuple-element.6.refs_0_, bf16[28,96,128]{2,1,0:T(8,128)(2,1)} %get-tuple-element.7.refs_1_, bf16[1152,128]{1,0:T(8,128)(2,1)} %bitcast.8, bf16[1152,128]{1,0:T(8,128)(2,1)} %bitcast.9, f32[1,128]{1,0:T(1,128)} %bitcast.10, ...), custom_call_target="tpu_custom_call" | custom-call | tf_op jit(solution)/shard_map/pallas_call | solution.py:492
  32.6 13.1 %shard_map.115 = f32[1,1]{1,0:T(1,128)} custom-call(f32[8,128]{1,0:T(8,128)} %get-tuple-element.9.refs_0_), custom_call_target="tpu_custom_call" | custom-call | tf_op jit(solution)/shard_map/pallas_call | solution.py:575

commit v3 on v2

--- a/solution.py
+++ b/solution.py
@@ -220,6 +220,8 @@
                 a, w = here_a + row[3], here_w + col[3]
                 if frame == mine and row[3] == 0 and col[3] == 0:
                     continue
+                if frame == other and col[3] != 0:
+                    continue
 
                 @pl.when(inside(a, w))
                 def _():
@@ -236,6 +238,8 @@
                 window_parts(mine, place, tile_rows, tile_cols)
             ):
                 a, w = here_a - row[3], here_w - col[3]
+                if place == other and col[3] != 0:
+                    continue
                 local = place == mine and row[3] == 0 and col[3] == 0
                 source = frames_ref.at[0, pl.ds(row[0], row[1]), pl.ds(col[0], col[1])]
                 target = wins[mine].at[pl.ds(row[2], row[1]), pl.ds(col[2], col[1])]
@@ -257,7 +261,7 @@
                     )
                 )
         own.start()
-        arrivals = []
+        arrivals, firsts, passed = [], [], []
         for frame in range(2):
             for slot, (row, col) in enumerate(
                 window_parts(frame, mine, tile_rows, tile_cols)
@@ -279,14 +283,32 @@
                     device_id_type=pl.DeviceIdType.MESH,
                 )
                 arrivals.append((inside(a, w), arrival))
+                if frame == other and col[3] == 0:
+                    firsts.append(arrivals.pop())
+                elif frame == other:
+                    out = (pl.ds(row[2], row[1]), pl.ds(SIDE + col[0], col[1]))
+                    onward = pltpu.make_async_remote_copy(
+                        src_ref=wins[frame].at[out],
+                        dst_ref=target,
+                        send_sem=send_sem.at[frame * 6 + slot],
+                        recv_sem=recv_sem.at[frame * 6 + slot],
+                        device_id=device(mine, here_a, here_w - col[3]),
+                        device_id_type=pl.DeviceIdType.MESH,
+                    )
+                    passed.append((row[3] != 0, inside(a, here_w - col[3]), onward))
                 pl.when(jnp.logical_not(inside(a, w)))(clear)
         pl.semaphore_wait(barrier, expected)
         for exists, copy in sends:
             pl.when(exists)(copy.start)
         own.wait()
+        for rim, (exists, arrival) in enumerate(firsts):
+            pl.when(exists)(arrival.wait_recv)
+            for of_rim, wanted, onward in passed:
+                if of_rim == bool(rim):
+                    pl.when(wanted)(onward.start)
         for exists, arrival in arrivals:
             pl.when(exists)(arrival.wait_recv)
-        for exists, copy in sends:
+        for exists, copy in sends + [entry[1:] for entry in passed]:
             pl.when(exists)(copy.wait_send)
 
     pl.when(here_t == 0)(lambda: branch(0))

time: 47.7 us -> 47.1 us (0.987)
  Pallas kernels: 45.1 us -> 44.5 us
    pallas_call x1, Pallas kernels: 18.2 us -> 15.6 us  [gather_windows(): pl.pallas_call(kernel, out_shape=shapes, in_specs=[pl.BlockSpec(memory_sp...]
    pallas_call x1, Pallas kernels: 13.1 us -> 15.1 us  [total_error(): pl.pallas_call(kernel, out_shape=jax.ShapeDtypeStruct((1, 1), jnp.float32...]
where the time goes in v3:
time: 47.1 us; the launch traced here: 46.9 us
  Pallas kernels  44.5 us (94%)
  between operations  2.4 us (5%)
    pallas_call x1, Pallas kernels, gather_windows(): pl.pallas_call(kernel, out_shape=shapes, in_specs=[pl.BlockSpec(memory_sp...  15.6 us
    pallas_call x1, Pallas kernels, total_error(): pl.pallas_call(kernel, out_shape=jax.ShapeDtypeStruct((1, 1), jnp.float32...  15.1 us
    pallas_call x1, Pallas kernels, predict(): pl.pallas_call(kernel, out_shape=[jax.ShapeDtypeStruct((tokens, channels)...  13.8 us

profile of v3, /device:TPU:0, one launch (start us, length us, event | category | flops | bytes accessed | tf_op | source)
XLA Modules:
  0.0 46.9 jit_solution(15017473246273816285)
XLA Ops:
  0.6 15.6 %shard_map.113 = (bf16[20,96,128]{2,1,0:T(8,128)(2,1)}, bf16[28,96,128]{2,1,0:T(8,128)(2,1)}) custom-call(bf16[1,32,64,128]{3,2,1,0:T(8,128)(2,1)} %refs_0_.1), custom_call_target="tpu_custom_call" | custom-call | tf_op jit(solution)/shard_map/pallas_call | solution.py:331
  16.2 13.8 %shard_map.114 = (bf16[2048,128]{1,0:T(8,128)(2,1)}, f32[8,128]{1,0:T(8,128)}) custom-call(bf16[20,96,128]{2,1,0:T(8,128)(2,1)} %get-tuple-element.6.refs_0_, bf16[28,96,128]{2,1,0:T(8,128)(2,1)} %get-tuple-element.7.refs_1_, bf16[1152,128]{1,0:T(8,128)(2,1)} %bitcast.8, bf16[1152,128]{1,0:T(8,128)(2,1)} %bitcast.9, f32[1,128]{1,0:T(1,128)} %bitcast.10, ...), custom_call_target="tpu_custom_call" | custom-call | tf_op jit(solution)/shard_map/pallas_call | solution.py:514
  30.0 15.1 %shard_map.115 = f32[1,1]{1,0:T(1,128)} custom-call(f32[8,128]{1,0:T(8,128)} %get-tuple-element.9.refs_0_), custom_call_target="tpu_custom_call" | custom-call | tf_op jit(solution)/shard_map/pallas_call | solution.py:597

commit v4 on v3

--- a/solution.py
+++ b/solution.py
@@ -233,7 +233,7 @@
                     )
 
         sends = []
-        for place in range(2):
+        for place in (other, mine):
             for slot, (row, col) in enumerate(
                 window_parts(mine, place, tile_rows, tile_cols)
             ):

time: 47.1 us -> 47.1 us (level)
  no operation moved by 1% of the time
where the time goes in v4:
time: 47.1 us; the launch traced here: 46.9 us
  Pallas kernels  44.5 us (94%)
  between operations  2.4 us (5%)
    pallas_call x1, Pallas kernels, gather_windows(): pl.pallas_call(kernel, out_shape=shapes, in_specs=[pl.BlockSpec(memory_sp...  15.6 us
    pallas_call x1, Pallas kernels, total_error(): pl.pallas_call(kernel, out_shape=jax.ShapeDtypeStruct((1, 1), jnp.float32...  15.1 us
    pallas_call x1, Pallas kernels, predict(): pl.pallas_call(kernel, out_shape=[jax.ShapeDtypeStruct((tokens, channels)...  13.8 us

profile of v4, /device:TPU:0, one launch (start us, length us, event | category | flops | bytes accessed | tf_op | source)
XLA Modules:
  0.0 46.9 jit_solution(4889402311321769819)
XLA Ops:
  0.6 15.6 %shard_map.113 = (bf16[20,96,128]{2,1,0:T(8,128)(2,1)}, bf16[28,96,128]{2,1,0:T(8,128)(2,1)}) custom-call(bf16[1,32,64,128]{3,2,1,0:T(8,128)(2,1)} %refs_0_.1), custom_call_target="tpu_custom_call" | custom-call | tf_op jit(solution)/shard_map/pallas_call | solution.py:331
  16.2 13.8 %shard_map.114 = (bf16[2048,128]{1,0:T(8,128)(2,1)}, f32[8,128]{1,0:T(8,128)}) custom-call(bf16[20,96,128]{2,1,0:T(8,128)(2,1)} %get-tuple-element.6.refs_0_, bf16[28,96,128]{2,1,0:T(8,128)(2,1)} %get-tuple-element.7.refs_1_, bf16[1152,128]{1,0:T(8,128)(2,1)} %bitcast.8, bf16[1152,128]{1,0:T(8,128)(2,1)} %bitcast.9, f32[1,128]{1,0:T(1,128)} %bitcast.10, ...), custom_call_target="tpu_custom_call" | custom-call | tf_op jit(solution)/shard_map/pallas_call | solution.py:514
  30.0 15.1 %shard_map.115 = f32[1,1]{1,0:T(1,128)} custom-call(f32[8,128]{1,0:T(8,128)} %get-tuple-element.9.refs_0_), custom_call_target="tpu_custom_call" | custom-call | tf_op jit(solution)/shard_map/pallas_call | solution.py:597
